TPU v7x, 256 devices: a whole 4x4x8 slice. The times are simulated.
256 devices in a mesh: gx: 32 (over z_hi, y, core), ga: 8 (over x, z_lo).
Axes of the slice: x: 4, y: 4, z: 8 (z_hi: 4, z_lo: 2; z = z_hi * 2 + z_lo), core: 2. Of those that a mesh axis runs over, the one named last changes fastest.
Arguments:
- velocity: float32 [6144, 32768], P('gx', 'ga'), may hold values from -12 to 12, as said below
- left_gram: float32 [25, 5], replicated, may hold values from -2.5 to 2.5
- right_gram: float32 [25, 5], replicated, may hold values from -2.5 to 2.5
Outputs:
- x_slope: float32 [6144, 32768], P('gx', 'ga')
- section_field: float32 [6144, 32768], P('gx', 'ga')
Inputs may be any that keep to these rules, and one draw needn't show every extreme that they name: velocity at the grid points.
All inputs are finite; a program needn't handle non-finite values.
Results may differ from a plain program's by a relative error of at most 0.000071.
Values sent between devices are 32-bit elements; how exact they have to be, the bound alone decides.
A program may use at most 64 MiB of HBM per device.

v0:
```python
import functools
import math

import jax
import jax.numpy as jnp
import ml_dtypes
import numpy as np
from jax import lax
from jax.experimental import pallas as pl
from jax.experimental.pallas import tpu as pltpu
from jax.sharding import PartitionSpec as P

MESH = pl.DeviceIdType.MESH
CONT = 25
DG = 5
NX = 6144
PERIOD = NX + CONT
ROWS = 192
PAIR = 2 * ROWS
LANES = 128
GX = 32
GA = 8
TALL = 768

courant = 0.5
epsilon = 1e-06


def derivative_table():
    shift = np.arange(2 * NX)[:, None] - np.arange(LANES)[None, :] - NX
    shift = shift % PERIOD
    shift = np.where(shift > PERIOD // 2, shift - PERIOD, shift)
    sign = np.where(shift % 2 == 0, 1.0, -1.0)
    angle = np.where(shift == 0, 1.0, shift * (np.pi / PERIOD))
    table = np.where(shift == 0, 0.0, (np.pi / PERIOD) * sign / np.sin(angle))
    high = table.astype(np.float32).astype(ml_dtypes.bfloat16)
    low = (table - high.astype(np.float64)).astype(np.float32).astype(ml_dtypes.bfloat16)
    return high, low


CHIPS = [(0, 0), (0, 1), (0, 3), (0, 2)]
CHIPS += [(dz, dy) for dy in (0, 1, 3, 2) for dz in (1, 3)]
CHIPS += [(2, dy) for dy in (0, 1, 3, 2)]
PEERS = [(dz, dy, dc) for dz, dy in CHIPS for dc in (0, 1)][1:]


def split(values):
    high = values.astype(jnp.bfloat16)
    low = (values - high.astype(jnp.float32)).astype(jnp.bfloat16)
    return jnp.concatenate([high, low], axis=1)


def kernel(
    v_hbm, high_hbm, low_hbm, left_ref, right_ref, slope_ref, rate_ref,
    v, high, low, lines, total, parts, tail, energy, energy_ga, energy_gx,
    local_sem, send_a, recv_a, send_b, recv_b, send_e, recv_e, send_f, recv_f,
):
    me = lax.axis_index("gx")
    group = lax.axis_index("ga")
    z, y, core = me // 8, (me // 2) % 4, me % 2

    def to(o):
        return ((z + o[0]) % 4) * 8 + ((y + o[1]) % 4) * 2 + (core + o[2]) % 2

    def source_chip(o):
        return ((z + 4 - o[0]) % 4) * 4 + (y + 4 - o[1]) % 4

    barrier = pltpu.get_barrier_semaphore()
    for o in PEERS:
        pl.semaphore_signal(barrier, inc=1, device_id={"gx": to(o)}, device_id_type=MESH)
    for k in range(1, GA):
        pl.semaphore_signal(
            barrier, inc=1, device_id={"ga": (group + k) % GA}, device_id_type=MESH
        )
    loads = [
        pltpu.make_async_copy(
            v_hbm.at[:, pl.ds(pl.multiple_of(me * LANES, LANES), LANES)],
            lines.at[pl.ds(pl.multiple_of(me * ROWS, ROWS), ROWS)],
            local_sem.at[0],
        ),
        pltpu.make_async_copy(high_hbm, high, local_sem.at[1]),
        pltpu.make_async_copy(low_hbm, low, local_sem.at[2]),
        pltpu.make_async_copy(v_hbm, v, local_sem.at[3]),
    ]
    for load in loads:
        load.start()
    pl.semaphore_wait(barrier, GX - 1 + GA - 1)

    forward = {}
    for k, o in enumerate(PEERS):
        there = to(o)
        forward[o] = pltpu.make_async_remote_copy(
            src_ref=v_hbm.at[:, pl.ds(pl.multiple_of(there * LANES, LANES), LANES)],
            dst_ref=lines.at[pl.ds(pl.multiple_of(me * ROWS, ROWS), ROWS)],
            send_sem=send_a.at[k],
            recv_sem=recv_a.at[k],
            device_id={"gx": there},
            device_id_type=MESH,
        )
        forward[o].start()

    loads[3].wait()

    def square_rows(i, sums):
        block = v[pl.ds(pl.multiple_of(i * 8, 8), 8), :]
        block = block * block
        for j in range(GX):
            sums = sums + block[:, j * LANES : (j + 1) * LANES]
        return sums

    energy[0] = lax.fori_loop(0, ROWS // 8, square_rows, jnp.zeros((8, LANES), jnp.float32))
    across_ga = []
    for k in range(1, GA):
        across_ga.append(
            pltpu.make_async_remote_copy(
                src_ref=energy.at[0],
                dst_ref=energy_ga.at[k],
                send_sem=send_e.at[k],
                recv_sem=recv_e.at[k],
                device_id={"ga": (group + k) % GA},
                device_id_type=MESH,
            )
        )
        across_ga[-1].start()

    def product(step_base, pieces, row, count, depth):
        tiles = [
            table[pl.ds(pl.multiple_of(row + (NX - 128 * j) - step_base, 128), count), :]
            for table in (high, low)
            for j in range(pieces)
        ]
        if depth:
            tiles += [table[pl.ds(pl.multiple_of(row, 128), count), :] for table in (high, low)]
        both = jnp.dot(
            jnp.concatenate(tiles, axis=1),
            parts[: len(tiles) * 128, :],
            preferred_element_type=jnp.float32,
        )
        return both[:, :LANES] + both[:, LANES:]

    def stage(base):
        pieces = split(lines[pl.ds(pl.multiple_of(base, 128), PAIR), :])
        parts[:PAIR, :] = pieces
        parts[PAIR : 2 * PAIR, :] = pieces

    for load in loads[:3]:
        load.wait()
    for i, chip in enumerate(CHIPS[:-1]):
        for dc in (0, 1):
            if (*chip, dc) in forward:
                forward[(*chip, dc)].wait_recv()
        base = source_chip(chip) * PAIR
        stage(base)

        def rows(r, carry, base=base, first=i == 0):
            row = pl.multiple_of(r * TALL, TALL)
            value = product(base, 3, row, TALL, False)
            here = pl.ds(row, TALL)
            total[here, :] = value if first else total[here, :] + value
            return carry

        lax.fori_loop(0, NX // TALL, rows, 0)
        if i == 4:
            for copy in across_ga:
                copy.wait()
            summed = energy[0]
            for k in range(1, GA):
                summed = summed + energy_ga[k]
            energy[1] = summed
            across_gx = []
            for k, o in enumerate(PEERS):
                across_gx.append(
                    pltpu.make_async_remote_copy(
                        src_ref=energy.at[1],
                        dst_ref=energy_gx.at[k],
                        send_sem=send_f.at[k],
                        recv_sem=recv_f.at[k],
                        device_id={"gx": to(o)},
                        device_id_type=MESH,
                    )
                )
                across_gx[-1].start()

    for dc in (0, 1):
        forward[(*CHIPS[-1], dc)].wait_recv()
    base = source_chip(CHIPS[-1]) * PAIR
    stage(base)
    ends = jnp.zeros((CONT, LANES), jnp.float32)
    for i in range(DG):
        ends = ends + left_ref[:, i : i + 1] * lines[i : i + 1, :]
    for i in range(DG):
        ends = ends + right_ref[:, i : i + 1] * lines[NX - DG + i : NX - DG + i + 1, :]
    tail[...] = jnp.zeros_like(tail)
    tail[:CONT, :] = ends
    pieces = split(tail[...])
    parts[2 * PAIR : 2 * PAIR + 128, :] = pieces
    parts[2 * PAIR + 128 :, :] = pieces

    mine = pl.ds(pl.multiple_of(me * LANES, LANES), LANES)
    back = []
    for chip in CHIPS[1:] + CHIPS[:1]:
        row = pl.multiple_of((to((*chip, 0)) // 2) * PAIR, PAIR)
        total[pl.ds(row, PAIR), :] = total[pl.ds(row, PAIR), :] + product(
            base, 3, row, PAIR, True
        )
        for dc in (0, 1):
            o = (*chip, dc)
            there = to(o)
            source = total.at[pl.ds(pl.multiple_of(there * ROWS, ROWS), ROWS)]
            if o == (0, 0, 0):
                own = pltpu.make_async_copy(source, slope_ref.at[:, mine], local_sem.at[0])
                own.start()
                continue
            k = PEERS.index(o)
            copy = pltpu.make_async_remote_copy(
                src_ref=source,
                dst_ref=slope_ref.at[:, mine],
                send_sem=send_b.at[k],
                recv_sem=recv_b.at[k],
                device_id={"gx": there},
                device_id_type=MESH,
            )
            copy.start()
            back.append(copy)

    for copy in across_gx:
        copy.wait()
    summed = energy[1]
    for k in range(GX - 1):
        summed = summed + energy_gx[k]
    count = NX * LANES * GX * GA
    mean_square = jnp.sum(summed, keepdims=True) / count
    rate = courant / jnp.sqrt(mean_square + epsilon)
    rate_ref[...] = jnp.broadcast_to(rate, (8, LANES))
    for o in PEERS:
        forward[o].wait_send()
    own.wait()
    for copy in back:
        copy.wait()


def per_device(velocity, left_gram, right_gram):
    high, low = derivative_table()
    anywhere = pl.BlockSpec(memory_space=pl.ANY)
    vmem = pl.BlockSpec(memory_space=pltpu.VMEM)
    dma = pltpu.SemaphoreType.DMA
    x_slope, rate = pl.pallas_call(
        kernel,
        out_shape=(
            jax.ShapeDtypeStruct((ROWS, LANES * GX), jnp.float32),
            jax.ShapeDtypeStruct((8, LANES), jnp.float32),
        ),
        in_specs=[anywhere, anywhere, anywhere, vmem, vmem],
        out_specs=(anywhere, vmem),
        scratch_shapes=[
            pltpu.VMEM((ROWS, LANES * GX), jnp.float32),
            pltpu.VMEM((2 * NX, LANES), jnp.bfloat16),
            pltpu.VMEM((2 * NX, LANES), jnp.bfloat16),
            pltpu.VMEM((NX, LANES), jnp.float32),
            pltpu.VMEM((NX, LANES), jnp.float32),
            pltpu.VMEM((2 * PAIR + 256, 2 * LANES), jnp.bfloat16),
            pltpu.VMEM((128, LANES), jnp.float32),
            pltpu.VMEM((2, 8, LANES), jnp.float32),
            pltpu.VMEM((GA, 8, LANES), jnp.float32),
            pltpu.VMEM((GX, 8, LANES), jnp.float32),
            dma((4,)),
            dma((GX - 1,)), dma((GX - 1,)), dma((GX - 1,)), dma((GX - 1,)),
            dma((GA,)), dma((GA,)), dma((GX - 1,)), dma((GX - 1,)),
        ],
        compiler_params=pltpu.CompilerParams(
            collective_id=0, has_side_effects=True, vmem_limit_bytes=48 * 2**20
        ),
        cost_estimate=pl.CostEstimate(
            flops=2 * NX * 2 * NX * 2 * LANES, bytes_accessed=16 * 2**20, transcendentals=0
        ),
        name="exchange_derivative",
    )(velocity, jnp.asarray(high), jnp.asarray(low), left_gram, right_gram)
    advect_rate = rate[0, 0]
    section_field = velocity - advect_rate * velocity * x_slope
    return (x_slope, section_field)


def solution(mesh):
    return jax.shard_map(
        per_device,
        mesh=mesh,
        in_specs=(P("gx", "ga"), P(), P()),
        out_specs=(P("gx", "ga"), P("gx", "ga")),
        check_vma=False,
    )
```

profile of v0, /device:TPU:1, one launch (start us, length us, event | category | flops | bytes accessed | tf_op | source)
XLA Modules:
  0.0 203.3 jit_solution(8398045708118562266)
XLA Ops:
  0.6 0.8 copy.7.left_ref
  1.4 0.8 copy.8.right_ref
  2.2 0.0 copy-start
  2.2 196.0 %exchange_derivative.1 = (f32[192,4096]{1,0:T(8,128)S(1)}, f32[8,128]{1,0:T(8,128)S(1)}) custom-call(f32[192,4096]{1,0:T(8,128)} %v_hbm.1, bf16[12288,128]{1,0:T(8,128)(2,1)} %constant.4.clone.high_hbm, bf16[12288,128]{1,0:T(8,128)(2,1)} %constant.5.clone.low_hbm, f32[25,5]{1,0:T(8,128)S(1)} %copy.7.left_ref, f32[25,5]{1,0:T(8,128)S(1)} %copy.8.right_ref), custom_call_target="tpu_custom_call" | custom-call | flops 38654705664 | bytes 16777216 | tf_op jit(solution)/shard_map/exchange_derivative/pallas_call | solution.py:247
  198.2 0.5 slice.3
  198.8 0.0 copy-done
  198.8 2.9 %multiply_subtract_fusion = f32[192,4096]{1,0:T(8,128)} fusion(f32[192,4096]{1,0:T(8,128)S(1)} %copy-done, f32[192,4096]{1,0:T(8,128)S(1)} %get-tuple-element.8, f32[]{:T(128)} %bitcast), kind=kLoop, calls=%fused_computation | loop fusion | flops 2359296 | bytes 9437188 | tf_op jit(solution)/shard_map/sub | solution.py:279
  201.7 1.7 copy.10
Async XLA Ops:
  2.2 196.6 %copy-start = (f32[192,4096]{1,0:T(8,128)S(1)}, f32[192,4096]{1,0:T(8,128)}, u32[]{:S(2)}) copy-start(f32[192,4096]{1,0:T(8,128)} %v_hbm.1) | copy-start | bytes 9437188
where the time goes:
time: 203 us
  Pallas kernels  196 us (97%)
  local copies, waits for them, and re-layouts  3.74 us (2%)
  other arithmetic  2.91 us (1%)
    pallas_call x1, Pallas kernels, per_device(): pl.pallas_call(kernel, out_shape=(jax.ShapeDtypeStruct((ROWS, LANES * GX)...  196 us

commit v1 on v0

--- a/solution.py
+++ b/solution.py
@@ -19,8 +19,9 @@
 PAIR = 2 * ROWS
 LANES = 128
 GX = 32
+CHIPS = 16
 GA = 8
-TALL = 768
+TALL = 1536
 
 courant = 0.5
 epsilon = 1e-06
@@ -38,10 +39,16 @@
     return high, low
 
 
-CHIPS = [(0, 0), (0, 1), (0, 3), (0, 2)]
-CHIPS += [(dz, dy) for dy in (0, 1, 3, 2) for dz in (1, 3)]
-CHIPS += [(2, dy) for dy in (0, 1, 3, 2)]
-PEERS = [(dz, dy, dc) for dz, dy in CHIPS for dc in (0, 1)][1:]
+AHEAD = 16
+
+
+def offset(i):
+    if isinstance(i, int):
+        return (0, i) if i < 4 else ((1, 3, 2)[(i - 4) % 3], (i - 4) // 3)
+    near = i < 4
+    k = jnp.maximum(i - 4, 0)
+    j = k % 3
+    return jnp.where(near, 0, 1 + 2 * j - 3 * (j // 2)), jnp.where(near, i, k // 3)
 
 
 def split(values):
@@ -59,15 +66,20 @@
     group = lax.axis_index("ga")
     z, y, core = me // 8, (me // 2) % 4, me % 2
 
-    def to(o):
-        return ((z + o[0]) % 4) * 8 + ((y + o[1]) % 4) * 2 + (core + o[2]) % 2
-
-    def source_chip(o):
-        return ((z + 4 - o[0]) % 4) * 4 + (y + 4 - o[1]) % 4
+    def to(dz, dy, dc):
+        return ((z + dz) % 4) * 8 + ((y + dy) % 4) * 2 + (core + dc) % 2
+
+    def source_chip(dz, dy):
+        return ((z + 4 - dz) % 4) * 4 + (y + 4 - dy) % 4
+
+    def cores(i):
+        return (1,) if isinstance(i, int) and i == 0 else (0, 1)
 
     barrier = pltpu.get_barrier_semaphore()
-    for o in PEERS:
-        pl.semaphore_signal(barrier, inc=1, device_id={"gx": to(o)}, device_id_type=MESH)
+    for i in range(CHIPS):
+        for dc in cores(i):
+            there = to(*offset(i), dc)
+            pl.semaphore_signal(barrier, inc=1, device_id={"gx": there}, device_id_type=MESH)
     for k in range(1, GA):
         pl.semaphore_signal(
             barrier, inc=1, device_id={"ga": (group + k) % GA}, device_id_type=MESH
@@ -86,18 +98,23 @@
         load.start()
     pl.semaphore_wait(barrier, GX - 1 + GA - 1)
 
-    forward = {}
-    for k, o in enumerate(PEERS):
-        there = to(o)
-        forward[o] = pltpu.make_async_remote_copy(
+    def forward(i, dc):
+        there = to(*offset(i), dc)
+        return pltpu.make_async_remote_copy(
             src_ref=v_hbm.at[:, pl.ds(pl.multiple_of(there * LANES, LANES), LANES)],
             dst_ref=lines.at[pl.ds(pl.multiple_of(me * ROWS, ROWS), ROWS)],
-            send_sem=send_a.at[k],
-            recv_sem=recv_a.at[k],
+            send_sem=send_a.at[2 * i + dc],
+            recv_sem=recv_a.at[2 * i + dc],
             device_id={"gx": there},
             device_id_type=MESH,
         )
-        forward[o].start()
+
+    def start_forward(i):
+        for dc in cores(i):
+            forward(i, dc).start()
+
+    for i in range(min(AHEAD, CHIPS)):
+        start_forward(i)
 
     loads[3].wait()
 
@@ -145,14 +162,14 @@
 
     for load in loads[:3]:
         load.wait()
-    for i, chip in enumerate(CHIPS[:-1]):
-        for dc in (0, 1):
-            if (*chip, dc) in forward:
-                forward[(*chip, dc)].wait_recv()
-        base = source_chip(chip) * PAIR
+
+    def work(i, first):
+        for dc in cores(i):
+            forward(i, dc).wait_recv()
+        base = source_chip(*offset(i)) * PAIR
         stage(base)
 
-        def rows(r, carry, base=base, first=i == 0):
+        def rows(r, carry):
             row = pl.multiple_of(r * TALL, TALL)
             value = product(base, 3, row, TALL, False)
             here = pl.ds(row, TALL)
@@ -160,30 +177,24 @@
             return carry
 
         lax.fori_loop(0, NX // TALL, rows, 0)
-        if i == 4:
-            for copy in across_ga:
-                copy.wait()
-            summed = energy[0]
-            for k in range(1, GA):
-                summed = summed + energy_ga[k]
-            energy[1] = summed
-            across_gx = []
-            for k, o in enumerate(PEERS):
-                across_gx.append(
-                    pltpu.make_async_remote_copy(
-                        src_ref=energy.at[1],
-                        dst_ref=energy_gx.at[k],
-                        send_sem=send_f.at[k],
-                        recv_sem=recv_f.at[k],
-                        device_id={"gx": to(o)},
-                        device_id_type=MESH,
-                    )
-                )
-                across_gx[-1].start()
+
+    work(0, True)
+
+    def work_and_send(i, carry):
+        start_forward(i + AHEAD - 1)
+        work(i, False)
+        return carry
+
+    def only_work(i, carry):
+        work(i, False)
+        return carry
+
+    lax.fori_loop(1, max(CHIPS + 1 - AHEAD, 1), work_and_send, 0)
+    lax.fori_loop(max(CHIPS + 1 - AHEAD, 1), CHIPS - 1, only_work, 0)
 
     for dc in (0, 1):
-        forward[(*CHIPS[-1], dc)].wait_recv()
-    base = source_chip(CHIPS[-1]) * PAIR
+        forward(CHIPS - 1, dc).wait_recv()
+    base = source_chip(*offset(CHIPS - 1)) * PAIR
     stage(base)
     ends = jnp.zeros((CONT, LANES), jnp.float32)
     for i in range(DG):
@@ -196,47 +207,77 @@
     parts[2 * PAIR : 2 * PAIR + 128, :] = pieces
     parts[2 * PAIR + 128 :, :] = pieces
 
+    for copy in across_ga:
+        copy.wait()
+    summed = energy[0]
+    for k in range(1, GA):
+        summed = summed + energy_ga[k]
+    energy[1] = summed
+    across_gx = []
+    for i in range(CHIPS):
+        for dc in cores(i):
+            across_gx.append(
+                pltpu.make_async_remote_copy(
+                    src_ref=energy.at[1],
+                    dst_ref=energy_gx.at[2 * i + dc],
+                    send_sem=send_f.at[2 * i + dc],
+                    recv_sem=recv_f.at[2 * i + dc],
+                    device_id={"gx": to(*offset(i), dc)},
+                    device_id_type=MESH,
+                )
+            )
+            across_gx[-1].start()
+
     mine = pl.ds(pl.multiple_of(me * LANES, LANES), LANES)
-    back = []
-    for chip in CHIPS[1:] + CHIPS[:1]:
-        row = pl.multiple_of((to((*chip, 0)) // 2) * PAIR, PAIR)
-        total[pl.ds(row, PAIR), :] = total[pl.ds(row, PAIR), :] + product(
-            base, 3, row, PAIR, True
-        )
-        for dc in (0, 1):
-            o = (*chip, dc)
-            there = to(o)
-            source = total.at[pl.ds(pl.multiple_of(there * ROWS, ROWS), ROWS)]
-            if o == (0, 0, 0):
-                own = pltpu.make_async_copy(source, slope_ref.at[:, mine], local_sem.at[0])
-                own.start()
-                continue
-            k = PEERS.index(o)
-            copy = pltpu.make_async_remote_copy(
-                src_ref=source,
-                dst_ref=slope_ref.at[:, mine],
-                send_sem=send_b.at[k],
-                recv_sem=recv_b.at[k],
-                device_id={"gx": there},
-                device_id_type=MESH,
-            )
-            copy.start()
-            back.append(copy)
+
+    def backward(i, dc):
+        there = to(*offset(i), dc)
+        return pltpu.make_async_remote_copy(
+            src_ref=total.at[pl.ds(pl.multiple_of(there * ROWS, ROWS), ROWS)],
+            dst_ref=slope_ref.at[:, mine],
+            send_sem=send_b.at[2 * i + dc],
+            recv_sem=recv_b.at[2 * i + dc],
+            device_id={"gx": there},
+            device_id_type=MESH,
+        )
+
+    def finish(i):
+        row = pl.multiple_of((to(*offset(i), 0) // 2) * PAIR, PAIR)
+        here = pl.ds(row, PAIR)
+        total[here, :] = total[here, :] + product(base, 3, row, PAIR, True)
+        for dc in cores(i):
+            backward(i, dc).start()
+
+    def finish_later(i, carry):
+        finish(CHIPS - i)
+        return carry
+
+    lax.fori_loop(1, CHIPS, finish_later, 0)
+    finish(0)
+    own = pltpu.make_async_copy(
+        total.at[pl.ds(pl.multiple_of(me * ROWS, ROWS), ROWS)], slope_ref.at[:, mine], local_sem.at[0]
+    )
+    own.start()
 
     for copy in across_gx:
         copy.wait()
     summed = energy[1]
-    for k in range(GX - 1):
+    for k in range(1, GX):
         summed = summed + energy_gx[k]
     count = NX * LANES * GX * GA
     mean_square = jnp.sum(summed, keepdims=True) / count
     rate = courant / jnp.sqrt(mean_square + epsilon)
     rate_ref[...] = jnp.broadcast_to(rate, (8, LANES))
-    for o in PEERS:
-        forward[o].wait_send()
     own.wait()
-    for copy in back:
-        copy.wait()
+
+    def wait_all(i, carry):
+        for dc in cores(i):
+            forward(i, dc).wait_send()
+            backward(i, dc).wait()
+        return carry
+
+    wait_all(0, 0)
+    lax.fori_loop(1, CHIPS, wait_all, 0)
 
 
 def per_device(velocity, left_gram, right_gram):
@@ -264,8 +305,8 @@
             pltpu.VMEM((GA, 8, LANES), jnp.float32),
             pltpu.VMEM((GX, 8, LANES), jnp.float32),
             dma((4,)),
-            dma((GX - 1,)), dma((GX - 1,)), dma((GX - 1,)), dma((GX - 1,)),
-            dma((GA,)), dma((GA,)), dma((GX - 1,)), dma((GX - 1,)),
+            dma((GX,)), dma((GX,)), dma((GX,)), dma((GX,)),
+            dma((GA,)), dma((GA,)), dma((GX,)), dma((GX,)),
         ],
         compiler_params=pltpu.CompilerParams(
             collective_id=0, has_side_effects=True, vmem_limit_bytes=48 * 2**20

time: 203 us -> 165 us (0.81)
  Pallas kernels: 196 us -> 158 us
    pallas_call x1, Pallas kernels: 196 us -> 158 us  [per_device(): pl.pallas_call(kernel, out_shape=(jax.ShapeDtypeStruct((ROWS, LANES * GX)...]
where the time goes in v1:
time: 165 us
  Pallas kernels  158 us (96%)
  local copies, waits for them, and re-layouts  3.74 us (2%)
  other arithmetic  2.91 us (2%)
    pallas_call x1, Pallas kernels, per_device(): pl.pallas_call(kernel, out_shape=(jax.ShapeDtypeStruct((ROWS, LANES * GX)...  158 us

profile of v1, /device:TPU:1, one launch (start us, length us, event | category | flops | bytes accessed | tf_op | source)
XLA Modules:
  0.0 164.9 jit_solution(12023161849864720506)
XLA Ops:
  0.6 0.8 copy.7.left_ref
  1.4 0.8 copy.8.right_ref
  2.2 0.0 copy-start
  2.2 157.6 %exchange_derivative.1 = (f32[192,4096]{1,0:T(8,128)S(1)}, f32[8,128]{1,0:T(8,128)S(1)}) custom-call(f32[192,4096]{1,0:T(8,128)} %v_hbm.1, bf16[12288,128]{1,0:T(8,128)(2,1)} %constant.4.clone.high_hbm, bf16[12288,128]{1,0:T(8,128)(2,1)} %constant.5.clone.low_hbm, f32[25,5]{1,0:T(8,128)S(1)} %copy.7.left_ref, f32[25,5]{1,0:T(8,128)S(1)} %copy.8.right_ref), custom_call_target="tpu_custom_call" | custom-call | flops 38654705664 | bytes 16777216 | tf_op jit(solution)/shard_map/exchange_derivative/pallas_call | solution.py:288
  159.8 0.5 slice.3
  160.3 0.0 copy-done
  160.3 2.9 %multiply_subtract_fusion = f32[192,4096]{1,0:T(8,128)} fusion(f32[192,4096]{1,0:T(8,128)S(1)} %copy-done, f32[192,4096]{1,0:T(8,128)S(1)} %get-tuple-element.8, f32[]{:T(128)} %bitcast), kind=kLoop, calls=%fused_computation | loop fusion | flops 2359296 | bytes 9437188 | tf_op jit(solution)/shard_map/sub | solution.py:320
  163.2 1.7 %copy.10 = f32[192,4096]{1,0:T(8,128)} copy(f32[192,4096]{1,0:T(8,128)S(1)} %get-tuple-element.8) | data formatting | bytes 6291456
Async XLA Ops:
  2.2 158.1 %copy-start = (f32[192,4096]{1,0:T(8,128)S(1)}, f32[192,4096]{1,0:T(8,128)}, u32[]{:S(2)}) copy-start(f32[192,4096]{1,0:T(8,128)} %v_hbm.1) | copy-start | bytes 9437188

commit v2 on v1

--- a/solution.py
+++ b/solution.py
@@ -39,16 +39,8 @@
     return high, low
 
 
-AHEAD = 16
-
-
 def offset(i):
-    if isinstance(i, int):
-        return (0, i) if i < 4 else ((1, 3, 2)[(i - 4) % 3], (i - 4) // 3)
-    near = i < 4
-    k = jnp.maximum(i - 4, 0)
-    j = k % 3
-    return jnp.where(near, 0, 1 + 2 * j - 3 * (j // 2)), jnp.where(near, i, k // 3)
+    return 2 * (i % 2) + i // 2 % 2, i // 4
 
 
 def split(values):
@@ -58,8 +50,8 @@
 
 
 def kernel(
-    v_hbm, high_hbm, low_hbm, left_ref, right_ref, slope_ref, rate_ref,
-    v, high, low, lines, total, parts, tail, energy, energy_ga, energy_gx,
+    v_hbm, high_hbm, low_hbm, left_hbm, right_hbm, slope_ref, section_ref,
+    v, left, right, high, low, lines, total, parts, tail, energy, energy_ga, energy_gx,
     local_sem, send_a, recv_a, send_b, recv_b, send_e, recv_e, send_f, recv_f,
 ):
     me = lax.axis_index("gx")
@@ -94,6 +86,10 @@
         pltpu.make_async_copy(low_hbm, low, local_sem.at[2]),
         pltpu.make_async_copy(v_hbm, v, local_sem.at[3]),
     ]
+    loads += [
+        pltpu.make_async_copy(left_hbm, left, local_sem.at[4]),
+        pltpu.make_async_copy(right_hbm, right, local_sem.at[5]),
+    ]
     for load in loads:
         load.start()
     pl.semaphore_wait(barrier, GX - 1 + GA - 1)
@@ -109,12 +105,15 @@
             device_id_type=MESH,
         )
 
-    def start_forward(i):
-        for dc in cores(i):
-            forward(i, dc).start()
-
-    for i in range(min(AHEAD, CHIPS)):
-        start_forward(i)
+    def send_to(owner):
+        def start_forward(i, carry):
+            forward(i, (core + owner) % 2).start()
+            return carry
+
+        lax.fori_loop(1, CHIPS, start_forward, 0)
+
+    forward(0, 1).start()
+    send_to(0)
 
     loads[3].wait()
 
@@ -140,6 +139,8 @@
         )
         across_ga[-1].start()
 
+    send_to(1)
+
     def product(step_base, pieces, row, count, depth):
         tiles = [
             table[pl.ds(pl.multiple_of(row + (NX - 128 * j) - step_base, 128), count), :]
@@ -160,7 +161,7 @@
         parts[:PAIR, :] = pieces
         parts[PAIR : 2 * PAIR, :] = pieces
 
-    for load in loads[:3]:
+    for load in loads[:3] + loads[4:]:
         load.wait()
 
     def work(i, first):
@@ -180,27 +181,30 @@
 
     work(0, True)
 
-    def work_and_send(i, carry):
-        start_forward(i + AHEAD - 1)
+    def work_later(i, carry):
         work(i, False)
         return carry
 
-    def only_work(i, carry):
-        work(i, False)
-        return carry
-
-    lax.fori_loop(1, max(CHIPS + 1 - AHEAD, 1), work_and_send, 0)
-    lax.fori_loop(max(CHIPS + 1 - AHEAD, 1), CHIPS - 1, only_work, 0)
+    lax.fori_loop(1, CHIPS - 1, work_later, 0)
 
     for dc in (0, 1):
         forward(CHIPS - 1, dc).wait_recv()
     base = source_chip(*offset(CHIPS - 1)) * PAIR
     stage(base)
-    ends = jnp.zeros((CONT, LANES), jnp.float32)
-    for i in range(DG):
-        ends = ends + left_ref[:, i : i + 1] * lines[i : i + 1, :]
-    for i in range(DG):
-        ends = ends + right_ref[:, i : i + 1] * lines[NX - DG + i : NX - DG + i + 1, :]
+    ends = lax.dot_general(
+        left[...],
+        lines[:DG, :],
+        (((0,), (0,)), ((), ())),
+        precision=lax.Precision.HIGHEST,
+        preferred_element_type=jnp.float32,
+    )
+    ends = ends + lax.dot_general(
+        right[...],
+        lines[NX - DG :, :],
+        (((0,), (0,)), ((), ())),
+        precision=lax.Precision.HIGHEST,
+        preferred_element_type=jnp.float32,
+    )
     tail[...] = jnp.zeros_like(tail)
     tail[:CONT, :] = ends
     pieces = split(tail[...])
@@ -249,7 +253,7 @@
             backward(i, dc).start()
 
     def finish_later(i, carry):
-        finish(CHIPS - i)
+        finish(i)
         return carry
 
     lax.fori_loop(1, CHIPS, finish_later, 0)
@@ -267,17 +271,47 @@
     count = NX * LANES * GX * GA
     mean_square = jnp.sum(summed, keepdims=True) / count
     rate = courant / jnp.sqrt(mean_square + epsilon)
-    rate_ref[...] = jnp.broadcast_to(rate, (8, LANES))
+
+    def section(i, dc):
+        there = ((z + 4 - offset(i)[0]) % 4) * 8 + ((y + 4 - offset(i)[1]) % 4) * 2 + (core + dc) % 2
+        here = pl.ds(pl.multiple_of(there * LANES, LANES), LANES)
+        block = v[:, here]
+        section_ref[:, here] = block - rate * block * slope_ref[:, here]
+
+    def receive(i, dc):
+        backward(i, dc).wait_recv()
+        section(i, dc)
+
     own.wait()
-
-    def wait_all(i, carry):
+    section(0, 0)
+    for sender in (0, 1):
+
+        def receive_later(i, carry, sender=sender):
+            receive(i, (core + sender) % 2)
+            return carry
+
+        lax.fori_loop(1, CHIPS, receive_later, 0)
+    receive(0, 1)
+
+    def wait_sent(i, carry):
         for dc in cores(i):
             forward(i, dc).wait_send()
-            backward(i, dc).wait()
+            backward(i, dc).wait_send()
         return carry
 
-    wait_all(0, 0)
-    lax.fori_loop(1, CHIPS, wait_all, 0)
+    wait_sent(0, 0)
+    lax.fori_loop(1, CHIPS, wait_sent, 0)
+
+
+def write_out(slope_vmem, section_vmem, slope_hbm, section_hbm, sem):
+    copies = [
+        pltpu.make_async_copy(slope_vmem, slope_hbm, sem.at[0]),
+        pltpu.make_async_copy(section_vmem, section_hbm, sem.at[1]),
+    ]
+    for copy in copies:
+        copy.start()
+    for copy in copies:
+        copy.wait()
 
 
 def per_device(velocity, left_gram, right_gram):
@@ -285,16 +319,16 @@
     anywhere = pl.BlockSpec(memory_space=pl.ANY)
     vmem = pl.BlockSpec(memory_space=pltpu.VMEM)
     dma = pltpu.SemaphoreType.DMA
-    x_slope, rate = pl.pallas_call(
+    block = jax.ShapeDtypeStruct((ROWS, LANES * GX), jnp.float32)
+    results = pl.pallas_call(
         kernel,
-        out_shape=(
-            jax.ShapeDtypeStruct((ROWS, LANES * GX), jnp.float32),
-            jax.ShapeDtypeStruct((8, LANES), jnp.float32),
-        ),
-        in_specs=[anywhere, anywhere, anywhere, vmem, vmem],
-        out_specs=(anywhere, vmem),
+        out_shape=(pltpu.VMEM(block.shape, block.dtype),) * 2,
+        in_specs=[pl.BlockSpec(memory_space=pltpu.HBM)] * 5,
+        out_specs=(vmem, vmem),
         scratch_shapes=[
             pltpu.VMEM((ROWS, LANES * GX), jnp.float32),
+            pltpu.VMEM((DG, CONT), jnp.float32),
+            pltpu.VMEM((DG, CONT), jnp.float32),
             pltpu.VMEM((2 * NX, LANES), jnp.bfloat16),
             pltpu.VMEM((2 * NX, LANES), jnp.bfloat16),
             pltpu.VMEM((NX, LANES), jnp.float32),
@@ -304,7 +338,7 @@
             pltpu.VMEM((2, 8, LANES), jnp.float32),
             pltpu.VMEM((GA, 8, LANES), jnp.float32),
             pltpu.VMEM((GX, 8, LANES), jnp.float32),
-            dma((4,)),
+            dma((6,)),
             dma((GX,)), dma((GX,)), dma((GX,)), dma((GX,)),
             dma((GA,)), dma((GA,)), dma((GX,)), dma((GX,)),
         ],
@@ -315,10 +349,16 @@
             flops=2 * NX * 2 * NX * 2 * LANES, bytes_accessed=16 * 2**20, transcendentals=0
         ),
         name="exchange_derivative",
-    )(velocity, jnp.asarray(high), jnp.asarray(low), left_gram, right_gram)
-    advect_rate = rate[0, 0]
-    section_field = velocity - advect_rate * velocity * x_slope
-    return (x_slope, section_field)
+    )(velocity, jnp.asarray(high), jnp.asarray(low), left_gram.T, right_gram.T)
+    return pl.pallas_call(
+        write_out,
+        out_shape=(block, block),
+        in_specs=[anywhere] * 2,
+        out_specs=(anywhere, anywhere),
+        scratch_shapes=[dma((2,))],
+        compiler_params=pltpu.CompilerParams(vmem_limit_bytes=2**20),
+        name="write_out",
+    )(*results)
 
 
 def solution(mesh):

time: 165 us -> 158 us (0.958)
  local copies, waits for them, and re-layouts: 3.74 us -> 0 us
  other arithmetic: 2.91 us -> 0 us
  Pallas kernels: 158 us -> 156 us
    unnamed x5 -> x0, local copies, waits for them, and re-layouts: 3.23 us -> none
    sub x1 -> x0, other arithmetic: 2.91 us -> none  [per_device(): section_field = velocity - advect_rate * velocity * x_slope]
    pallas_call x1 -> x2, Pallas kernels: 158 us -> 156 us  [the longest x1 153 us: per_device(): pl.pallas_call(kernel, out_shape=(pltpu.VMEM(block.shape, block.dtype),)...]
where the time goes in v2:
time: 158 us; the launch traced here: 157 us
  Pallas kernels  156 us (99%)
    pallas_call x1, Pallas kernels, per_device(): pl.pallas_call(kernel, out_shape=(pltpu.VMEM(block.shape, block.dtype),)...  153 us

profile of v2, /device:TPU:1, one launch (start us, length us, event | category | flops | bytes accessed | tf_op | source)
XLA Modules:
  0.0 156.8 jit_solution(1249718520051048546)
XLA Ops:
  0.6 153.5 %exchange_derivative.1 = (f32[192,4096]{1,0:T(8,128)S(1)}, f32[192,4096]{1,0:T(8,128)S(1)}) custom-call(f32[192,4096]{1,0:T(8,128)} %v_hbm.1, bf16[12288,128]{1,0:T(8,128)(2,1)} %constant.4.clone.high_hbm, bf16[12288,128]{1,0:T(8,128)(2,1)} %constant.5.clone.low_hbm, f32[5,25]{1,0:T(8,128)} %bitcast.2, f32[5,25]{1,0:T(8,128)} %bitcast.3), custom_call_target="tpu_custom_call" | custom-call | flops 38654705664 | bytes 16777216 | tf_op jit(solution)/shard_map/exchange_derivative/pallas_call | solution.py:323
  154.1 2.7 %write_out.1 = (f32[192,4096]{1,0:T(8,128)}, f32[192,4096]{1,0:T(8,128)}) custom-call(f32[192,4096]{1,0:T(8,128)S(1)} %get-tuple-element.4.slope_vmem, f32[192,4096]{1,0:T(8,128)S(1)} %get-tuple-element.5.section_vmem), custom_call_target="tpu_custom_call" | custom-call | tf_op jit(solution)/shard_map/write_out/pallas_call | solution.py:353

commit v3 on v2

--- a/solution.py
+++ b/solution.py
@@ -20,6 +20,7 @@
 LANES = 128
 GX = 32
 CHIPS = 16
+MIDWAY = 10
 GA = 8
 TALL = 1536
 
@@ -185,7 +186,33 @@
         work(i, False)
         return carry
 
-    lax.fori_loop(1, CHIPS - 1, work_later, 0)
+    lax.fori_loop(1, MIDWAY, work_later, 0)
+
+    def exchange(value, slot, offsets):
+        energy[slot] = value
+        copies = []
+        for k, (dz, dy, dc) in offsets:
+            copies.append(
+                pltpu.make_async_remote_copy(
+                    src_ref=energy.at[slot],
+                    dst_ref=energy_gx.at[k],
+                    send_sem=send_f.at[k],
+                    recv_sem=recv_f.at[k],
+                    device_id={"gx": to(dz, dy, dc)},
+                    device_id_type=MESH,
+                )
+            )
+            copies[-1].start()
+        return copies
+
+    for copy in across_ga:
+        copy.wait()
+    summed = energy[0]
+    for k in range(1, GA):
+        summed = summed + energy_ga[k]
+    across_y = exchange(summed, 1, [(k, (0, k // 2, k % 2)) for k in range(1, 8)])
+
+    lax.fori_loop(MIDWAY, CHIPS - 1, work_later, 0)
 
     for dc in (0, 1):
         forward(CHIPS - 1, dc).wait_recv()
@@ -211,27 +238,6 @@
     parts[2 * PAIR : 2 * PAIR + 128, :] = pieces
     parts[2 * PAIR + 128 :, :] = pieces
 
-    for copy in across_ga:
-        copy.wait()
-    summed = energy[0]
-    for k in range(1, GA):
-        summed = summed + energy_ga[k]
-    energy[1] = summed
-    across_gx = []
-    for i in range(CHIPS):
-        for dc in cores(i):
-            across_gx.append(
-                pltpu.make_async_remote_copy(
-                    src_ref=energy.at[1],
-                    dst_ref=energy_gx.at[2 * i + dc],
-                    send_sem=send_f.at[2 * i + dc],
-                    recv_sem=recv_f.at[2 * i + dc],
-                    device_id={"gx": to(*offset(i), dc)},
-                    device_id_type=MESH,
-                )
-            )
-            across_gx[-1].start()
-
     mine = pl.ds(pl.multiple_of(me * LANES, LANES), LANES)
 
     def backward(i, dc):
@@ -256,17 +262,24 @@
         finish(i)
         return carry
 
-    lax.fori_loop(1, CHIPS, finish_later, 0)
+    lax.fori_loop(1, CHIPS // 2, finish_later, 0)
+    for copy in across_y:
+        copy.wait()
+    summed = energy[1]
+    for k in range(1, 8):
+        summed = summed + energy_gx[k]
+    across_z = exchange(summed, 2, [(8 + k, (k, 0, 0)) for k in range(1, 4)])
+    lax.fori_loop(CHIPS // 2, CHIPS, finish_later, 0)
     finish(0)
     own = pltpu.make_async_copy(
         total.at[pl.ds(pl.multiple_of(me * ROWS, ROWS), ROWS)], slope_ref.at[:, mine], local_sem.at[0]
     )
     own.start()
 
-    for copy in across_gx:
+    for copy in across_z:
         copy.wait()
-    summed = energy[1]
-    for k in range(1, GX):
+    summed = energy[2]
+    for k in range(9, 12):
         summed = summed + energy_gx[k]
     count = NX * LANES * GX * GA
     mean_square = jnp.sum(summed, keepdims=True) / count
@@ -335,12 +348,12 @@
             pltpu.VMEM((NX, LANES), jnp.float32),
             pltpu.VMEM((2 * PAIR + 256, 2 * LANES), jnp.bfloat16),
             pltpu.VMEM((128, LANES), jnp.float32),
-            pltpu.VMEM((2, 8, LANES), jnp.float32),
+            pltpu.VMEM((3, 8, LANES), jnp.float32),
             pltpu.VMEM((GA, 8, LANES), jnp.float32),
-            pltpu.VMEM((GX, 8, LANES), jnp.float32),
+            pltpu.VMEM((12, 8, LANES), jnp.float32),
             dma((6,)),
             dma((GX,)), dma((GX,)), dma((GX,)), dma((GX,)),
-            dma((GA,)), dma((GA,)), dma((GX,)), dma((GX,)),
+            dma((GA,)), dma((GA,)), dma((12,)), dma((12,)),
         ],
         compiler_params=pltpu.CompilerParams(
             collective_id=0, has_side_effects=True, vmem_limit_bytes=48 * 2**20

time: 158 us -> 156 us (0.987)
  Pallas kernels: 156 us -> 154 us
    pallas_call x1, Pallas kernels: 153 us -> 151 us  [per_device(): pl.pallas_call(kernel, out_shape=(pltpu.VMEM(block.shape, block.dtype),)...]
where the time goes in v3:
time: 156 us; the launch traced here: 154 us
  Pallas kernels  154 us (99%)
    pallas_call x1, Pallas kernels, per_device(): pl.pallas_call(kernel, out_shape=(pltpu.VMEM(block.shape, block.dtype),)...  151 us

profile of v3, /device:TPU:1, one launch (start us, length us, event | category | flops | bytes accessed | tf_op | source)
XLA Modules:
  0.0 154.4 jit_solution(209549011541824699)
XLA Ops:
  0.6 151.1 %exchange_derivative.1 = (f32[192,4096]{1,0:T(8,128)S(1)}, f32[192,4096]{1,0:T(8,128)S(1)}) custom-call(f32[192,4096]{1,0:T(8,128)} %v_hbm.1, bf16[12288,128]{1,0:T(8,128)(2,1)} %constant.4.clone.high_hbm, bf16[12288,128]{1,0:T(8,128)(2,1)} %constant.5.clone.low_hbm, f32[5,25]{1,0:T(8,128)} %bitcast.2, f32[5,25]{1,0:T(8,128)} %bitcast.3), custom_call_target="tpu_custom_call" | custom-call | flops 38654705664 | bytes 16777216 | tf_op jit(solution)/shard_map/exchange_derivative/pallas_call | solution.py:336
  151.7 2.7 %write_out.1 = (f32[192,4096]{1,0:T(8,128)}, f32[192,4096]{1,0:T(8,128)}) custom-call(f32[192,4096]{1,0:T(8,128)S(1)} %get-tuple-element.4.slope_vmem, f32[192,4096]{1,0:T(8,128)S(1)} %get-tuple-element.5.section_vmem), custom_call_target="tpu_custom_call" | custom-call | tf_op jit(solution)/shard_map/write_out/pallas_call | solution.py:366

commit v4 on v3

--- a/solution.py
+++ b/solution.py
@@ -21,6 +21,7 @@
 GX = 32
 CHIPS = 16
 MIDWAY = 10
+PARTS = 4
 GA = 8
 TALL = 1536
 
@@ -292,7 +293,8 @@
         section_ref[:, here] = block - rate * block * slope_ref[:, here]
 
     def receive(i, dc):
-        backward(i, dc).wait_recv()
+        forward(i, dc).wait_send()
+        backward(i, dc).wait()
         section(i, dc)
 
     own.wait()
@@ -306,20 +308,17 @@
         lax.fori_loop(1, CHIPS, receive_later, 0)
     receive(0, 1)
 
-    def wait_sent(i, carry):
-        for dc in cores(i):
-            forward(i, dc).wait_send()
-            backward(i, dc).wait_send()
-        return carry
-
-    wait_sent(0, 0)
-    lax.fori_loop(1, CHIPS, wait_sent, 0)
-
 
 def write_out(slope_vmem, section_vmem, slope_hbm, section_hbm, sem):
+    part = ROWS // PARTS
     copies = [
-        pltpu.make_async_copy(slope_vmem, slope_hbm, sem.at[0]),
-        pltpu.make_async_copy(section_vmem, section_hbm, sem.at[1]),
+        pltpu.make_async_copy(
+            source.at[pl.ds(k * part, part)], target.at[pl.ds(k * part, part)], sem.at[PARTS * n + k]
+        )
+        for k in range(PARTS)
+        for n, (source, target) in enumerate(
+            ((slope_vmem, slope_hbm), (section_vmem, section_hbm))
+        )
     ]
     for copy in copies:
         copy.start()
@@ -368,7 +367,7 @@
         out_shape=(block, block),
         in_specs=[anywhere] * 2,
         out_specs=(anywhere, anywhere),
-        scratch_shapes=[dma((2,))],
+        scratch_shapes=[dma((2 * PARTS,))],
         compiler_params=pltpu.CompilerParams(vmem_limit_bytes=2**20),
         name="write_out",
     )(*results)

time: 156 us -> 156 us (level)
  no operation moved by 1% of the time
where the time goes in v4:
time: 156 us; the launch traced here: 154 us
  Pallas kernels  154 us (99%)
    pallas_call x1, Pallas kernels, per_device(): pl.pallas_call(kernel, out_shape=(pltpu.VMEM(block.shape, block.dtype),)...  151 us

profile of v4, /device:TPU:1, one launch (start us, length us, event | category | flops | bytes accessed | tf_op | source)
XLA Modules:
  0.0 154.3 jit_solution(16104098136885718053)
XLA Ops:
  0.6 150.9 %exchange_derivative.1 = (f32[192,4096]{1,0:T(8,128)S(1)}, f32[192,4096]{1,0:T(8,128)S(1)}) custom-call(f32[192,4096]{1,0:T(8,128)} %v_hbm.1, bf16[12288,128]{1,0:T(8,128)(2,1)} %constant.4.clone.high_hbm, bf16[12288,128]{1,0:T(8,128)(2,1)} %constant.5.clone.low_hbm, f32[5,25]{1,0:T(8,128)} %bitcast.2, f32[5,25]{1,0:T(8,128)} %bitcast.3), custom_call_target="tpu_custom_call" | custom-call | flops 38654705664 | bytes 16777216 | tf_op jit(solution)/shard_map/exchange_derivative/pallas_call | solution.py:335
  151.6 2.7 %write_out.1 = (f32[192,4096]{1,0:T(8,128)}, f32[192,4096]{1,0:T(8,128)}) custom-call(f32[192,4096]{1,0:T(8,128)S(1)} %get-tuple-element.4.slope_vmem, f32[192,4096]{1,0:T(8,128)S(1)} %get-tuple-element.5.section_vmem), custom_call_target="tpu_custom_call" | custom-call | tf_op jit(solution)/shard_map/write_out/pallas_call | solution.py:365
